TPU v7x, 256 devices: a whole 4x4x8 slice. The times are simulated.
256 devices in a mesh: grp: 4 (over x_lo, core), blk: 64 (over y, z, x_hi).
Axes of the slice: x: 4 (x_hi: 2, x_lo: 2; x = x_hi * 2 + x_lo), y: 4, z: 8, core: 2. Of those that a mesh axis runs over, the one named last changes fastest.
Arguments:
- image_emb: float32 [131072, 1152], P(('grp', 'blk')), may hold values from -0.2 to 0.2
- text_emb: float32 [131072, 1152], P(('grp', 'blk')), may hold values from -0.2 to 0.2
- logit_scale: float32 [1], replicated, may hold values from 8 to 32
- logit_bias: float32 [1], replicated, may hold values from -4 to -1
Outputs:
- image_grad: float32 [131072, 1152], P(('grp', 'blk'))
- text_grad: float32 [131072, 1152], P(('grp', 'blk'))
All inputs are finite; a program needn't handle non-finite values.
Results may differ from a plain program's by a relative error of at most 0.006.
Values may be sent and summed in bfloat16 or wider, within the bound.
A program may use at most 64 MiB of HBM per device.

v0:
```python
import jax
import jax.numpy as jnp
from jax import lax
from jax.sharding import PartitionSpec as P

epsilon = 1e-06


def shifted(value, axis, by):
    devices = lax.axis_size(axis)
    return lax.ppermute(value, axis, [(i, (i + by) % devices) for i in range(devices)])


def normalize(values):
    inverse = lax.rsqrt(jnp.sum(values * values, axis=-1, keepdims=True) + epsilon)
    return (values * inverse, inverse)


def project_back(unit, inverse, accum):
    return inverse * (accum - unit * jnp.sum(unit * accum, axis=-1, keepdims=True))


def tile_weights(images, texts, scale_value, bias_value, diagonal):
    logits = jnp.dot(images, texts.T, preferred_element_type=jnp.float32) * scale_value + bias_value
    if diagonal:
        rows_idx = lax.broadcasted_iota(jnp.int32, logits.shape, 0)
        cols_idx = lax.broadcasted_iota(jnp.int32, logits.shape, 1)
        labels = jnp.where(rows_idx == cols_idx, 1.0, -1.0).astype(jnp.float32)
    else:
        labels = -jnp.ones_like(logits)
    grads = -labels * jax.nn.sigmoid(-labels * logits)
    return (scale_value * grads).astype(jnp.bfloat16)


def local(image_emb, text_emb, logit_scale, logit_bias):
    image_unit, image_inv = normalize(image_emb)
    text_unit, text_inv = normalize(text_emb)
    image_bf = image_unit.astype(jnp.bfloat16)
    text_bf = text_unit.astype(jnp.bfloat16)
    scale_value = logit_scale[0]
    bias_value = logit_bias[0]
    weights = tile_weights(image_bf, text_bf, scale_value, bias_value, True)
    image_acc = jnp.dot(weights, text_bf, preferred_element_type=jnp.float32)
    text_acc = jnp.dot(weights.T, image_bf, preferred_element_type=jnp.float32)
    partials = []
    for offset in (1, 2, 3):
        visitor = shifted(text_bf, "blk", offset)
        weights = tile_weights(image_bf, visitor, scale_value, bias_value, False)
        image_acc = image_acc + jnp.dot(weights, visitor, preferred_element_type=jnp.float32)
        partials.append(jnp.dot(weights.T, image_bf, preferred_element_type=jnp.float32))
    for offset in (1, 2, 3):
        text_acc = text_acc + shifted(
            partials[offset - 1].astype(jnp.bfloat16), "blk", -offset
        ).astype(jnp.float32)
    visitor = shifted(text_bf, "grp", 1)
    weights = tile_weights(image_bf, visitor, scale_value, bias_value, False)
    image_acc = image_acc + jnp.dot(weights, visitor, preferred_element_type=jnp.float32)
    remote_part = jnp.dot(weights.T, image_bf, preferred_element_type=jnp.float32)
    text_acc = text_acc + shifted(remote_part.astype(jnp.bfloat16), "grp", -1).astype(
        remote_part.dtype
    )
    return (
        project_back(image_unit, image_inv, image_acc),
        project_back(text_unit, text_inv, text_acc),
    )


def solution(mesh):
    in_specs = (P(("grp", "blk"), None), P(("grp", "blk"), None), P(), P())
    out_specs = (P(("grp", "blk"), None), P(("grp", "blk"), None))
    return jax.shard_map(local, mesh=mesh, in_specs=in_specs, out_specs=out_specs, check_vma=False)
```

profile of v0, /device:TPU:1, one launch (start us, length us, event | category | flops | bytes accessed | tf_op | source)
XLA Modules:
  0.0 192.4 jit_solution(8777756385238898833)
XLA Ops:
  0.6 0.0 copy-start.1
  0.6 2.0 %multiply_reduce_fusion.2 = f32[512]{0:T(512)S(1)} fusion(f32[512,1152]{1,0:T(8,128)} %param.5), kind=kLoop, calls=%fused_computation.13 | loop fusion | flops 1179136 | bytes 2361344 | tf_op jit(solution)/shard_map/reduce_sum | solution.py:15
  2.7 0.3 copy-done.1
  3.0 0.0 copy-start
  3.0 0.2 multiply_convert_fusion
  3.2 2.7 %collective-permute-start.3 = (bf16[512,1152]{1,0:T(8,128)(2,1)S(1)}, bf16[512,1152]{1,0:T(8,128)(2,1)S(1)}, u32[]{:S(2)}, u32[]{:S(2)}) collective-permute-start(bf16[512,1152]{1,0:T(8,128)(2,1)S(1)} %multiply_convert_fusion), channel_id=1, source_target_pairs={{0,64},{64,128},{128,192},{192,0},{1,65},{65,129},{129,193},{193,1... | collective-permute-start | bytes 3538952 | tf_op jit(solution)/shard_map/ppermute | solution.py:11
  5.9 3.8 %collective-permute-start.2 = (bf16[512,1152]{1,0:T(8,128)(2,1)S(1)}, bf16[512,1152]{1,0:T(8,128)(2,1)S(1)}, u32[]{:S(2)}, u32[]{:S(2)}) collective-permute-start(bf16[512,1152]{1,0:T(8,128)(2,1)S(1)} %multiply_convert_fusion), channel_id=1, source_target_pairs={{0,3},{1,4},{2,5},{3,6},{4,7},{5,8},{6,9},{7,10},{8,11},{9,12},{10... | collective-permute-start | bytes 3538952 | tf_op jit(solution)/shard_map/ppermute | solution.py:11
  9.7 1.9 collective-permute-start
  11.6 1.6 collective-permute-start.1
  13.2 0.0 copy-done
  13.2 0.2 multiply_reduce_fusion.3
  14.8 0.2 multiply_convert_fusion.1
  15.0 1.1 fusion.34
  16.0 0.8 fusion.39
  16.9 34.6 %collective-permute-done.3 = bf16[512,1152]{1,0:T(8,128)(2,1)S(1)} collective-permute-done((bf16[512,1152]{1,0:T(8,128)(2,1)S(1)}, bf16[512,1152]{1,0:T(8,128)(2,1)S(1)}, u32[]{:S(2)}, u32[]{:S(2)}) %collective-permute-start.3) | collective-permute-done | bytes 1179680 | tf_op jit(solution)/shard_map/ppermute | solution.py:11
  51.5 1.0 fusion.35
  52.5 0.9 convolution_convert_fusion
  53.4 4.9 %collective-permute-start.7 = (bf16[512,1152]{1,0:T(8,128)(2,1)S(1)}, bf16[512,1152]{1,0:T(8,128)(2,1)S(1)}, u32[]{:S(2)}, u32[]{:S(2)}) collective-permute-start(bf16[512,1152]{1,0:T(8,128)(2,1)S(1)} %convolution_convert_fusion), channel_id=1, source_target_pairs={{0,192},{64,0},{128,64},{192,128},{1,193},{65,1},{129,65},{193,129... | collective-permute-start | bytes 3538952 | tf_op jit(solution)/shard_map/ppermute | solution.py:11
  58.3 0.0 collective-permute-done.2
  58.3 1.0 fusion.36
  59.4 0.9 convolution_convert_fusion.1
  60.2 0.1 collective-permute-start.6
  60.3 20.4 %collective-permute-done.1 = bf16[512,1152]{1,0:T(8,128)(2,1)S(1)} collective-permute-done((bf16[512,1152]{1,0:T(8,128)(2,1)S(1)}, bf16[512,1152]{1,0:T(8,128)(2,1)S(1)}, u32[]{:S(2)}, u32[]{:S(2)}) %collective-permute-start.1) | collective-permute-done | bytes 1179680 | tf_op jit(solution)/shard_map/ppermute | solution.py:11
  80.7 1.0 fusion.37
  81.8 0.9 convolution_convert_fusion.2
  82.6 0.3 collective-permute-start.5
  82.9 26.4 %collective-permute-done = bf16[512,1152]{1,0:T(8,128)(2,1)S(1)} collective-permute-done((bf16[512,1152]{1,0:T(8,128)(2,1)S(1)}, bf16[512,1152]{1,0:T(8,128)(2,1)S(1)}, u32[]{:S(2)}, u32[]{:S(2)}) %collective-permute-start) | collective-permute-done | bytes 1179680 | tf_op jit(solution)/shard_map/ppermute | solution.py:11
  109.3 1.0 fusion.38
  110.3 0.9 convolution_convert_fusion.3
  111.2 33.7 %collective-permute-start.4 = (bf16[512,1152]{1,0:T(8,128)(2,1)S(1)}, bf16[512,1152]{1,0:T(8,128)(2,1)S(1)}, u32[]{:S(2)}, u32[]{:S(2)}) collective-permute-start(bf16[512,1152]{1,0:T(8,128)(2,1)S(1)} %convolution_convert_fusion.3), channel_id=1, source_target_pairs={{0,63},{1,0},{2,1},{3,2},{4,3},{5,4},{6,5},{7,6},{8,7},{9,8},{10,9... | collective-permute-start | bytes 3538952 | tf_op jit(solution)/shard_map/ppermute | solution.py:11
  144.8 0.8 fusion.41
  145.7 0.8 fusion.40
  146.5 0.9 convolution_add_fusion.1
  147.4 1.3 multiply_reduce_fusion.1
  148.7 1.8 subtract_multiply_fusion.1
  150.6 0.0 collective-permute-done.7
  150.6 0.0 collective-permute-done.6
  150.6 0.0 collective-permute-done.5
  150.6 37.9 %collective-permute-done.4 = bf16[512,1152]{1,0:T(8,128)(2,1)S(1)} collective-permute-done((bf16[512,1152]{1,0:T(8,128)(2,1)S(1)}, bf16[512,1152]{1,0:T(8,128)(2,1)S(1)}, u32[]{:S(2)}, u32[]{:S(2)}) %collective-permute-start.4) | collective-permute-done | bytes 1179680 | tf_op jit(solution)/shard_map/ppermute | solution.py:11
  188.5 1.6 multiply_reduce_fusion
  190.1 2.3 %subtract_multiply_fusion = f32[512,1152]{1,0:T(8,128)} fusion(f32[512,1152]{1,0:T(8,128)S(1)} %copy-done.1, f32[512]{0:T(512)S(1)} %get-tuple-element.4, f32[512]{0:T(512)S(1)} %add_rsqrt_fusion, bf16[512,1152]{1,0:T(8,128)(2,1)S(1)} %collective-permute-done.7, bf16[512,1152]{1,0:T(8,128)(2,1)S(1)} %collective-permute-done.6, ...), kind=kLoop, calls=%fused_computation.8 | loop fusion | flops 7077888 | bytes 11800576 | tf_op jit(solution)/shard_map/mul | solution.py:20
  (2 shorter events, 0.0 us)
Async XLA Ops:
  0.6 2.4 %copy-start.1 = (f32[512,1152]{1,0:T(8,128)S(1)}, f32[512,1152]{1,0:T(8,128)}, u32[]{:S(2)}) copy-start(f32[512,1152]{1,0:T(8,128)} %param.5) | copy-start | bytes 7077892
  3.0 10.2 %copy-start = (f32[512,1152]{1,0:T(8,128)S(1)}, f32[512,1152]{1,0:T(8,128)}, u32[]{:S(2)}) copy-start(f32[512,1152]{1,0:T(8,128)} %param.4) | copy-start | bytes 7077892
  3.2 48.3 %collective-permute-start.3 = (bf16[512,1152]{1,0:T(8,128)(2,1)S(1)}, bf16[512,1152]{1,0:T(8,128)(2,1)S(1)}, u32[]{:S(2)}, u32[]{:S(2)}) collective-permute-start(bf16[512,1152]{1,0:T(8,128)(2,1)S(1)} %multiply_convert_fusion), channel_id=1, source_target_pairs={{0,64},{64,128},{128,192},{192,0},{1,65},{65,129},{129,193},{193,1... | collective-permute-start | bytes 3538952 | tf_op jit(solution)/shard_map/ppermute | solution.py:11
  5.9 52.4 %collective-permute-start.2 = (bf16[512,1152]{1,0:T(8,128)(2,1)S(1)}, bf16[512,1152]{1,0:T(8,128)(2,1)S(1)}, u32[]{:S(2)}, u32[]{:S(2)}) collective-permute-start(bf16[512,1152]{1,0:T(8,128)(2,1)S(1)} %multiply_convert_fusion), channel_id=1, source_target_pairs={{0,3},{1,4},{2,5},{3,6},{4,7},{5,8},{6,9},{7,10},{8,11},{9,12},{10... | collective-permute-start | bytes 3538952 | tf_op jit(solution)/shard_map/ppermute | solution.py:11
  9.7 99.6 %collective-permute-start = (bf16[512,1152]{1,0:T(8,128)(2,1)S(1)}, bf16[512,1152]{1,0:T(8,128)(2,1)S(1)}, u32[]{:S(2)}, u32[]{:S(2)}) collective-permute-start(bf16[512,1152]{1,0:T(8,128)(2,1)S(1)} %multiply_convert_fusion), channel_id=1, source_target_pairs={{0,1},{1,2},{2,3},{3,4},{4,5},{5,6},{6,7},{7,8},{8,9},{9,10},{10,1... | collective-permute-start | bytes 3538952 | tf_op jit(solution)/shard_map/ppermute | solution.py:11
  11.6 69.2 %collective-permute-start.1 = (bf16[512,1152]{1,0:T(8,128)(2,1)S(1)}, bf16[512,1152]{1,0:T(8,128)(2,1)S(1)}, u32[]{:S(2)}, u32[]{:S(2)}) collective-permute-start(bf16[512,1152]{1,0:T(8,128)(2,1)S(1)} %multiply_convert_fusion), channel_id=1, source_target_pairs={{0,2},{1,3},{2,4},{3,5},{4,6},{5,7},{6,8},{7,9},{8,10},{9,11},{10,... | collective-permute-start | bytes 3538952 | tf_op jit(solution)/shard_map/ppermute | solution.py:11
  53.4 97.2 %collective-permute-start.7 = (bf16[512,1152]{1,0:T(8,128)(2,1)S(1)}, bf16[512,1152]{1,0:T(8,128)(2,1)S(1)}, u32[]{:S(2)}, u32[]{:S(2)}) collective-permute-start(bf16[512,1152]{1,0:T(8,128)(2,1)S(1)} %convolution_convert_fusion), channel_id=1, source_target_pairs={{0,192},{64,0},{128,64},{192,128},{1,193},{65,1},{129,65},{193,129... | collective-permute-start | bytes 3538952 | tf_op jit(solution)/shard_map/ppermute | solution.py:11
  60.2 90.3 %collective-permute-start.6 = (bf16[512,1152]{1,0:T(8,128)(2,1)S(1)}, bf16[512,1152]{1,0:T(8,128)(2,1)S(1)}, u32[]{:S(2)}, u32[]{:S(2)}) collective-permute-start(bf16[512,1152]{1,0:T(8,128)(2,1)S(1)} %convolution_convert_fusion.1), channel_id=1, source_target_pairs={{0,61},{1,62},{2,63},{3,0},{4,1},{5,2},{6,3},{7,4},{8,5},{9,6},{10... | collective-permute-start | bytes 3538952 | tf_op jit(solution)/shard_map/ppermute | solution.py:11
  82.6 67.9 %collective-permute-start.5 = (bf16[512,1152]{1,0:T(8,128)(2,1)S(1)}, bf16[512,1152]{1,0:T(8,128)(2,1)S(1)}, u32[]{:S(2)}, u32[]{:S(2)}) collective-permute-start(bf16[512,1152]{1,0:T(8,128)(2,1)S(1)} %convolution_convert_fusion.2), channel_id=1, source_target_pairs={{0,62},{1,63},{2,0},{3,1},{4,2},{5,3},{6,4},{7,5},{8,6},{9,7},{10,... | collective-permute-start | bytes 3538952 | tf_op jit(solution)/shard_map/ppermute | solution.py:11
  111.2 77.3 %collective-permute-start.4 = (bf16[512,1152]{1,0:T(8,128)(2,1)S(1)}, bf16[512,1152]{1,0:T(8,128)(2,1)S(1)}, u32[]{:S(2)}, u32[]{:S(2)}) collective-permute-start(bf16[512,1152]{1,0:T(8,128)(2,1)S(1)} %convolution_convert_fusion.3), channel_id=1, source_target_pairs={{0,63},{1,0},{2,1},{3,2},{4,3},{5,4},{6,5},{7,6},{8,7},{9,8},{10,9... | collective-permute-start | bytes 3538952 | tf_op jit(solution)/shard_map/ppermute | solution.py:11
where the time goes:
time: 194 us; the launch traced here: 192 us
  waiting for transfers between devices  119 us (61%)
  starting transfers between devices  49 us (25%)
  matrix products  15 us (8%)
  other arithmetic  6.84 us (4%)
  between operations  2.06 us (1%)
    ppermute x8, waiting for transfers between devices, shifted(): lax.ppermute(value, axis, [(i, (i + by) % devices) for i in range(devices)])  119 us
    ppermute x8, starting transfers between devices, shifted(): lax.ppermute(value, axis, [(i, (i + by) % devices) for i in range(devices)])  49 us
    dot_general x5, matrix products, tile_weights(): jnp.dot(images, texts.T, preferred_element_type=jnp.float32) * scale_value  5.14 us
    mul x2, other arithmetic, project_back(): inverse * (accum - unit * jnp.sum(unit * accum, axis=-1, keepdims=True))  4.16 us
    dot_general x4, matrix products, local(): jnp.dot(weights, visitor, preferred_element_type=jnp.float32)  3.9 us
  transfers between devices with their start and end apart: 8, of which 4 were waited for; matrix products, arithmetic and copies ran while one was open for 8% of the time, Pallas kernels for 0%

commit v1 on v0

v1 whole, which is shorter than its diff:
```python
import functools

import jax
import jax.numpy as jnp
from jax import lax
from jax.experimental import pallas as pl
from jax.experimental.pallas import tpu as pltpu
from jax.sharding import PartitionSpec as P

EPSILON = 1e-6
MESH = pl.DeviceIdType.MESH
F32 = jnp.float32
BF16 = jnp.bfloat16
TEXT_PARTS = 8
IMAGE_PARTS = 4


def product(a, b, contract):
    return lax.dot_general(a, b, ((contract[:1], contract[1:]), ((), ())), preferred_element_type=F32)


def kernel(
    n_grp, n_blk, rows, scale_ref, bias_ref, image_hbm, text_hbm, image_out, text_out,
    image32, text32, image_inv, text_inv, texts, images, weights, text_acc, image_acc, group_acc,
    text_send, image_send, group_send, text_back, image_back, relay_back, group_back,
    load_sem, store_sem,
    direct_s, group_s, relay_s, image_s, text_back_s, image_back_s, group_back_s,
    visit_r, group_r, image_r, text_back_r, image_back_r, relay_back_r, group_back_r,
):
    g, c = lax.axis_index("grp"), lax.axis_index("blk")
    even = lax.rem(g, 2) == 0
    odd = jnp.logical_not(even)
    tr, ir = rows // TEXT_PARTS, rows // IMAGE_PARTS
    scale, bias = scale_ref[0], bias_ref[0]

    def at(dg, dc):
        return (lax.rem(g + (dg + n_grp), n_grp), lax.rem(c + (dc + n_blk), n_blk))

    def text_rows(k, base=0):
        return pl.ds(pl.multiple_of(base + k * tr, tr), tr)

    def image_rows(k, base=0):
        return pl.ds(pl.multiple_of(base + k * ir, ir), ir)

    def remote(src, dst, send, recv, k, device):
        return pltpu.make_async_remote_copy(
            src_ref=src, dst_ref=dst, send_sem=send.at[k], recv_sem=recv.at[k],
            device_id=device, device_id_type=MESH,
        )

    own, visit, guest = 0, rows, 2 * rows

    def direct_copy(k):
        return remote(texts.at[text_rows(k)], texts.at[text_rows(k, visit)], direct_s, visit_r, k, at(0, 1))

    def group_copy(k):
        return remote(texts.at[text_rows(k)], texts.at[text_rows(k, guest)], group_s, group_r, k, at(1, 0))

    def relay_copy(k):
        return remote(
            texts.at[text_rows(k, guest)], texts.at[text_rows(k, visit)], relay_s, visit_r, k, at(-1, 1)
        )

    def image_copy(k):
        return remote(images.at[image_rows(k)], images.at[image_rows(k, rows)], image_s, image_r, k, at(0, -2))

    def text_back_copy(k):
        return remote(text_send.at[text_rows(k)], text_back.at[text_rows(k)], text_back_s, text_back_r, k, at(0, -1))

    def via_back_copy(k):
        return remote(
            text_send.at[text_rows(k)], relay_back.at[text_rows(k)], text_back_s, relay_back_r, k, at(1, -1)
        )

    def sum_back_copy(k):
        return remote(group_send.at[text_rows(k)], text_back.at[text_rows(k)], group_back_s, text_back_r, k, at(-1, 0))

    def group_back_copy(k):
        return remote(
            group_send.at[text_rows(k)], group_back.at[text_rows(k)], group_back_s, group_back_r, k, at(-1, 0)
        )

    def image_back_copy(k):
        return remote(
            image_send.at[image_rows(k)], image_back.at[image_rows(k)], image_back_s, image_back_r, k, at(0, 2)
        )

    def text_load(k):
        return pltpu.make_async_copy(text_hbm.at[text_rows(k)], text32.at[text_rows(k)], load_sem.at[0, k])

    def image_load(k):
        return pltpu.make_async_copy(image_hbm.at[image_rows(k)], image32.at[image_rows(k)], load_sem.at[1, k])

    def text_store(k):
        return pltpu.make_async_copy(text32.at[text_rows(k)], text_out.at[text_rows(k)], store_sem.at[0, k])

    def image_store(k):
        return pltpu.make_async_copy(image32.at[image_rows(k)], image_out.at[image_rows(k)], store_sem.at[1, k])

    barrier = pltpu.get_barrier_semaphore()

    def greet(partners):
        for partner in partners:
            pl.semaphore_signal(barrier, inc=1, device_id=at(*partner), device_id_type=MESH)

    common = ((0, 2), (0, -2), (1, 0), (-1, 0))
    pl.when(even)(lambda: greet(common + ((0, 1), (0, -1), (-1, 1))))
    pl.when(odd)(lambda: greet(common + ((1, -1),)))

    for k in range(TEXT_PARTS):
        text_load(k).start()
        if k < IMAGE_PARTS:
            image_load(k).start()

    def normalize(raw, inv, out, where):
        values = raw[where, :]
        inverse = lax.rsqrt(jnp.sum(values * values, axis=-1, keepdims=True) + EPSILON)
        inv[where, :] = inverse
        out[where, :] = (values * inverse).astype(BF16)

    def text_ready(k):
        text_load(k).wait()
        normalize(text32, text_inv, texts, text_rows(k))

    def text_go(k):
        pl.when(even)(lambda: direct_copy(k).start())
        group_copy(k).start()

    text_ready(0)
    pl.semaphore_wait(barrier, jnp.where(even, 7, 5))
    text_go(0)

    def image_first(k, _):
        image_load(k).wait()
        normalize(image32, image_inv, images, image_rows(k))
        image_copy(k).start()

    def text_first(k, _):
        text_ready(k)
        text_go(k)

    image_first(0, None)
    lax.fori_loop(1, TEXT_PARTS, lambda k, _: text_first(k, _), None)
    lax.fori_loop(1, IMAGE_PARTS, lambda k, _: image_first(k, _), None)

    def weigh(logit, diagonal=None):
        logit = logit * scale + bias
        if diagonal is None:
            return (scale / (1.0 + jnp.exp(-logit))).astype(BF16)
        sign = jnp.where(diagonal, -1.0, 1.0).astype(F32)
        return ((sign * scale) / (1.0 + jnp.exp(-sign * logit))).astype(BF16)

    def group_step(k, _):
        mine, theirs = text_rows(k), text_rows(k, guest)
        logit = product(texts[mine, :], images[:rows, :], (1, 1))
        down = lax.broadcasted_iota(jnp.int32, logit.shape, 0) + k * tr
        across = lax.broadcasted_iota(jnp.int32, logit.shape, 1)
        weights[mine, :rows] = weigh(logit, down == across)

        group_copy(k).wait_recv()
        pl.when(even)(lambda: relay_copy(k).start())
        weight = weigh(product(texts[theirs, :], images[:rows, :], (1, 1)))
        weights[theirs, :rows] = weight
        part = product(weight, images[:rows, :], (1, 0))

        @pl.when(even)
        def _():
            group_acc[mine, :] = part

        @pl.when(odd)
        def _():
            group_send[mine, :] = part.astype(BF16)
            group_back_copy(k).start()

    lax.fori_loop(0, TEXT_PARTS, group_step, None)

    def visit_step(k, _):
        image_copy(k).wait_recv()
        there = image_rows(k, rows)
        weights[:rows, there] = weigh(product(texts[:rows, :], images[there, :], (1, 1)))
        for part in range(TEXT_PARTS // IMAGE_PARTS):
            direct_copy(k * (TEXT_PARTS // IMAGE_PARTS) + part).wait_recv()
        here = image_rows(k, visit)
        weights[here, :rows] = weigh(product(texts[here, :], images[:rows, :], (1, 1)))

    lax.fori_loop(0, IMAGE_PARTS, visit_step, None)

    def corner_step(k, _):
        here = image_rows(k, visit)
        weights[here, rows:] = weigh(product(texts[here, :], images[rows:, :], (1, 1)))

    lax.fori_loop(0, IMAGE_PARTS, corner_step, None)

    def back_step(k, _):
        for part in range(TEXT_PARTS // IMAGE_PARTS):
            j = k * (TEXT_PARTS // IMAGE_PARTS) + part
            text_send[text_rows(j), :] = product(weights[text_rows(j, visit), :], images[...], (1, 0)).astype(BF16)
            pl.when(even)(lambda: text_back_copy(j).start())
            pl.when(odd)(lambda: via_back_copy(j).start())
            if part == 0:
                there = image_rows(k, rows)
                image_send[image_rows(k), :] = product(
                    weights[: 2 * rows, there], texts[: 2 * rows, :], (0, 0)
                ).astype(BF16)
                image_back_copy(k).start()

    lax.fori_loop(0, IMAGE_PARTS, back_step, None)

    def rest_step(k, _):
        here = image_rows(k)
        text_acc[here, :] = product(weights[here, :], images[...], (1, 0))
        image_acc[here, :] = product(weights[:, here], texts[...], (0, 0))

    lax.fori_loop(0, IMAGE_PARTS, rest_step, None)

    def project(raw, inv, accum, where):
        inverse = inv[where, :]
        unit = raw[where, :] * inverse
        raw[where, :] = inverse * (accum - unit * jnp.sum(unit * accum, axis=-1, keepdims=True))

    def last_step(k, _):
        for part in range(TEXT_PARTS // IMAGE_PARTS):
            j = k * (TEXT_PARTS // IMAGE_PARTS) + part
            here = text_rows(j)

            @pl.when(even)
            def _():
                via_back_copy(j).wait_recv()
                group_send[here, :] = (group_acc[here, :] + relay_back[here, :].astype(F32)).astype(BF16)
                sum_back_copy(j).start()
                group_back_copy(j).wait_recv()
                text_acc[here, :] += group_back[here, :].astype(F32)

            text_back_copy(j).wait_recv()
            project(text32, text_inv, text_acc[here, :] + text_back[here, :].astype(F32), here)
            text_store(j).start()
        here = image_rows(k)
        image_back_copy(k).wait_recv()
        project(image32, image_inv, image_acc[here, :] + image_back[here, :].astype(F32), here)
        image_store(k).start()

    lax.fori_loop(0, IMAGE_PARTS, last_step, None)

    def text_done(k, _):
        group_copy(k).wait_send()
        text_back_copy(k).wait_send()
        group_back_copy(k).wait_send()

        @pl.when(even)
        def _():
            direct_copy(k).wait_send()
            relay_copy(k).wait_send()

        text_store(k).wait()

    lax.fori_loop(0, TEXT_PARTS, text_done, None)

    def image_done(k, _):
        image_copy(k).wait_send()
        image_back_copy(k).wait_send()
        image_store(k).wait()

    lax.fori_loop(0, IMAGE_PARTS, image_done, None)


def local(n_grp, n_blk, image_emb, text_emb, logit_scale, logit_bias):
    rows, width = image_emb.shape
    whole, bf = pltpu.VMEM((rows, width), F32), pltpu.VMEM((rows, width), BF16)
    text_sem, image_sem = pltpu.SemaphoreType.DMA((TEXT_PARTS,)), pltpu.SemaphoreType.DMA((IMAGE_PARTS,))
    out = jax.ShapeDtypeStruct((rows, width), F32)
    tile = 2 * rows * rows * width
    return pl.pallas_call(
        functools.partial(kernel, n_grp, n_blk, rows),
        out_shape=(out, out),
        in_specs=[pl.BlockSpec(memory_space=pltpu.SMEM)] * 2 + [pl.BlockSpec(memory_space=pl.ANY)] * 2,
        out_specs=(pl.BlockSpec(memory_space=pl.ANY),) * 2,
        scratch_shapes=[
            whole, whole, pltpu.VMEM((rows, 1), F32), pltpu.VMEM((rows, 1), F32),
            pltpu.VMEM((3 * rows, width), BF16), pltpu.VMEM((2 * rows, width), BF16),
            pltpu.VMEM((3 * rows, 2 * rows), BF16), whole, whole, whole,
            bf, bf, bf, bf, bf, bf, bf,
            pltpu.SemaphoreType.DMA((2, TEXT_PARTS)), pltpu.SemaphoreType.DMA((2, TEXT_PARTS)),
            text_sem, text_sem, text_sem, image_sem, text_sem, image_sem, text_sem,
            text_sem, text_sem, image_sem, text_sem, image_sem, text_sem, text_sem,
        ],
        cost_estimate=pl.CostEstimate(
            flops=15 * tile, bytes_accessed=16 * rows * width, transcendentals=5 * rows * rows
        ),
        compiler_params=pltpu.CompilerParams(
            collective_id=0, has_side_effects=True, vmem_limit_bytes=48 * 2**20
        ),
        name="contrast",
    )(logit_scale, logit_bias, image_emb, text_emb)


def solution(mesh):
    blocks = P(("grp", "blk"), None)
    return jax.shard_map(
        functools.partial(local, mesh.shape["grp"], mesh.shape["blk"]),
        mesh=mesh,
        in_specs=(blocks, blocks, P(), P()),
        out_specs=(blocks, blocks),
        check_vma=False,
    )
```

time: 194 us -> 83.5 us (0.43)
  waiting for transfers between devices: 119 us -> 0 us
  Pallas kernels: 0 us -> 78.6 us
  starting transfers between devices: 49 us -> 0 us
  matrix products: 15 us -> 0 us
  other arithmetic: 6.84 us -> 0 us
  local copies, waits for them, and re-layouts: 0.32 us -> 2.81 us
    ppermute x8 -> x0, waiting for transfers between devices: 119 us -> none  [shifted(): lax.ppermute(value, axis, [(i, (i + by) % devices) for i in range(devices)])]
    pallas_call x0 -> x1, Pallas kernels: none -> 78.6 us  [local(): pl.pallas_call(functools.partial(kernel, n_grp, n_blk, rows), out_shape=(...]
    ppermute x8 -> x0, starting transfers between devices: 49 us -> none  [shifted(): lax.ppermute(value, axis, [(i, (i + by) % devices) for i in range(devices)])]
    dot_general x15 -> x0, matrix products: 15 us -> none  [the longest x5 5.14 us: tile_weights(): jnp.dot(images, texts.T, preferred_element_type=jnp.float32) * scale_value]
    mul x2 -> x0, other arithmetic: 4.16 us -> none  [project_back(): inverse * (accum - unit * jnp.sum(unit * accum, axis=-1, keepdims=True))]
    unnamed x4 -> x2, local copies, waits for them, and re-layouts: 0.32 us -> 2.81 us
    reduce_sum x2 -> x0, other arithmetic: 2.27 us -> none  [normalize(): jnp.sum(values * values, axis=-1, keepdims=True) + epsilon]
  transfers between devices with their start and end apart: 8 -> 0, of which waited for: 4 -> 0; matrix products, arithmetic and copies ran while one was open for 8% -> 0% of each run, Pallas kernels for 0% -> 0%
where the time goes in v1:
time: 83.5 us; the launch traced here: 83.4 us
  Pallas kernels  78.6 us (94%)
  local copies, waits for them, and re-layouts  2.81 us (3%)
  between operations  1.93 us (2%)
    pallas_call x1, Pallas kernels, local(): pl.pallas_call(functools.partial(kernel, n_grp, n_blk, rows), out_shape=(...  78.6 us
    unnamed x2, local copies, waits for them, and re-layouts  2.81 us

profile of v1, /device:TPU:1, one launch (start us, length us, event | category | flops | bytes accessed | tf_op | source)
XLA Modules:
  0.0 83.4 jit_solution(11903616262488969266)
XLA Ops:
  1.9 78.6 %contrast.1 = (f32[512,1152]{1,0:T(8,128)S(1)}, f32[512,1152]{1,0:T(8,128)S(1)}) custom-call(f32[1]{0:T(128)S(6)} %copy.8.scale_ref, f32[1]{0:T(128)S(6)} %copy.9.bias_ref, f32[512,1152]{1,0:T(8,128)} %image_hbm.1, f32[512,1152]{1,0:T(8,128)} %text_hbm.1), custom_call_target="tpu_custom_call" | custom-call | flops 9059696640 | bytes 9437184 | tf_op jit(solution)/shard_map/contrast/pallas_call | solution.py:272
  80.6 1.4 %copy.10 = f32[512,1152]{1,0:T(8,128)} copy(f32[512,1152]{1,0:T(8,128)S(1)} %get-tuple-element.4) | data formatting | bytes 4718592
  82.0 1.4 %copy.11 = f32[512,1152]{1,0:T(8,128)} copy(f32[512,1152]{1,0:T(8,128)S(1)} %get-tuple-element.5) | data formatting | bytes 4718592

commit v2 on v1

--- a/solution.py
+++ b/solution.py
@@ -13,6 +13,8 @@
 BF16 = jnp.bfloat16
 TEXT_PARTS = 8
 IMAGE_PARTS = 4
+AHEAD = 2
+IMAGE_HOLD = 3
 
 
 def product(a, b, contract):
@@ -25,11 +27,13 @@
     text_send, image_send, group_send, text_back, image_back, relay_back, group_back,
     load_sem, store_sem,
     direct_s, group_s, relay_s, image_s, text_back_s, image_back_s, group_back_s,
-    visit_r, group_r, image_r, text_back_r, image_back_r, relay_back_r, group_back_r,
+    visit_r, group_r, image_r, text_back_r, image_back_r, relay_back_r, group_back_r, ack_sem, go_sem,
 ):
     g, c = lax.axis_index("grp"), lax.axis_index("blk")
     even = lax.rem(g, 2) == 0
     odd = jnp.logical_not(even)
+    even_place = lax.rem(c, 2) == 0
+    odd_place = jnp.logical_not(even_place)
     tr, ir = rows // TEXT_PARTS, rows // IMAGE_PARTS
     scale, bias = scale_ref[0], bias_ref[0]
 
@@ -99,18 +103,17 @@
 
     barrier = pltpu.get_barrier_semaphore()
 
-    def greet(partners):
+    def signal(semaphore, partners):
         for partner in partners:
-            pl.semaphore_signal(barrier, inc=1, device_id=at(*partner), device_id_type=MESH)
-
-    common = ((0, 2), (0, -2), (1, 0), (-1, 0))
-    pl.when(even)(lambda: greet(common + ((0, 1), (0, -1), (-1, 1))))
-    pl.when(odd)(lambda: greet(common + ((1, -1),)))
-
-    for k in range(TEXT_PARTS):
-        text_load(k).start()
-        if k < IMAGE_PARTS:
-            image_load(k).start()
+            pl.semaphore_signal(semaphore, inc=1, device_id=at(*partner), device_id_type=MESH)
+
+    pl.when(even)(lambda: signal(barrier, ((1, 0), (-1, 0), (0, -1), (0, -2))))
+    pl.when(odd)(lambda: signal(barrier, ((1, 0), (-1, 0), (0, -2), (1, -1), (-1, -2))))
+
+    for k in range(IMAGE_PARTS):
+        for j in range(TEXT_PARTS // IMAGE_PARTS):
+            text_load(k * (TEXT_PARTS // IMAGE_PARTS) + j).start()
+        image_load(k).start()
 
     def normalize(raw, inv, out, where):
         values = raw[where, :]
@@ -123,25 +126,38 @@
         normalize(text32, text_inv, texts, text_rows(k))
 
     def text_go(k):
-        pl.when(even)(lambda: direct_copy(k).start())
         group_copy(k).start()
 
     text_ready(0)
-    pl.semaphore_wait(barrier, jnp.where(even, 7, 5))
+    pl.semaphore_wait(barrier, jnp.where(even, 6, 3))
     text_go(0)
-
-    def image_first(k, _):
+    pl.when(even)(lambda: signal(ack_sem, ((0, 1), (0, 2), (-1, 1))))
+    pl.when(odd)(lambda: signal(ack_sem, ((0, 2),)))
+
+    def each(parts, step):
+        lax.fori_loop(0, parts, lambda k, _: step(k), None)
+
+    def image_ready(k):
         image_load(k).wait()
         normalize(image32, image_inv, images, image_rows(k))
-        image_copy(k).start()
-
-    def text_first(k, _):
+
+    def text_first(k):
         text_ready(k)
         text_go(k)
 
-    image_first(0, None)
-    lax.fori_loop(1, TEXT_PARTS, lambda k, _: text_first(k, _), None)
-    lax.fori_loop(1, IMAGE_PARTS, lambda k, _: image_first(k, _), None)
+    several = TEXT_PARTS // IMAGE_PARTS
+
+    def both_first(k, _):
+        each(several, lambda j: text_first(k * several + j))
+        image_ready(k)
+        pl.when(odd)(lambda: image_copy(k).start())
+
+    image_ready(0)
+    pl.semaphore_wait(ack_sem, 2)
+    pl.when(odd)(lambda: image_copy(0).start())
+    lax.fori_loop(1, several, lambda k, _: text_first(k), None)
+    lax.fori_loop(1, IMAGE_PARTS, both_first, None)
+
 
     def weigh(logit, diagonal=None):
         logit = logit * scale + bias
@@ -150,106 +166,160 @@
         sign = jnp.where(diagonal, -1.0, 1.0).astype(F32)
         return ((sign * scale) / (1.0 + jnp.exp(-sign * logit))).astype(BF16)
 
-    def group_step(k, _):
-        mine, theirs = text_rows(k), text_rows(k, guest)
-        logit = product(texts[mine, :], images[:rows, :], (1, 1))
-        down = lax.broadcasted_iota(jnp.int32, logit.shape, 0) + k * tr
-        across = lax.broadcasted_iota(jnp.int32, logit.shape, 1)
-        weights[mine, :rows] = weigh(logit, down == across)
-
+    def score(text_at, text_n, image_at, image_n):
+        t, i = pl.ds(text_at, text_n), pl.ds(image_at, image_n)
+        weights[t, i] = weigh(product(texts[t, :], images[i, :], (1, 1)))
+
+    logit = product(texts[:rows, :], images[:rows, :], (1, 1))
+    down = lax.broadcasted_iota(jnp.int32, logit.shape, 0)
+    across = lax.broadcasted_iota(jnp.int32, logit.shape, 1)
+    weights[:rows, :rows] = weigh(logit, down == across)
+
+    half = rows // 2
+
+    def guest_half(h):
+        score(guest + h * half, half, 0, rows)
+        return product(weights[pl.ds(guest + h * half, half), :rows], images[:rows, :], (1, 0))
+
+    def images_arrive(h):
+        for k in range(h * IMAGE_PARTS // 2, (h + 1) * IMAGE_PARTS // 2):
+            image_copy(k).wait_recv()
+
+    def texts_arrive(h):
+        for k in range(h * TEXT_PARTS // 2, (h + 1) * TEXT_PARTS // 2):
+            direct_copy(k).wait_recv()
+
+    def text_return(h):
+        block = pl.ds(visit + h * half, half)
+        text_send[pl.ds(h * half, half), :] = product(weights[block, :], images[...], (1, 0)).astype(BF16)
+
+    def image_return(h):
+        block = pl.ds(rows + h * half, half)
+        image_send[pl.ds(h * half, half), :] = product(
+            weights[: 2 * rows, block], texts[: 2 * rows, :], (0, 0)
+        ).astype(BF16)
+
+    def relay_step(k, _):
         group_copy(k).wait_recv()
-        pl.when(even)(lambda: relay_copy(k).start())
-        weight = weigh(product(texts[theirs, :], images[:rows, :], (1, 1)))
-        weights[theirs, :rows] = weight
-        part = product(weight, images[:rows, :], (1, 0))
-
-        @pl.when(even)
+        relay_copy(k).start()
+
+        @pl.when(k == IMAGE_HOLD)
         def _():
-            group_acc[mine, :] = part
-
-        @pl.when(odd)
-        def _():
-            group_send[mine, :] = part.astype(BF16)
-            group_back_copy(k).start()
-
-    lax.fori_loop(0, TEXT_PARTS, group_step, None)
-
-    def visit_step(k, _):
-        image_copy(k).wait_recv()
-        there = image_rows(k, rows)
-        weights[:rows, there] = weigh(product(texts[:rows, :], images[there, :], (1, 1)))
-        for part in range(TEXT_PARTS // IMAGE_PARTS):
-            direct_copy(k * (TEXT_PARTS // IMAGE_PARTS) + part).wait_recv()
-        here = image_rows(k, visit)
-        weights[here, :rows] = weigh(product(texts[here, :], images[:rows, :], (1, 1)))
-
-    lax.fori_loop(0, IMAGE_PARTS, visit_step, None)
-
-    def corner_step(k, _):
-        here = image_rows(k, visit)
-        weights[here, rows:] = weigh(product(texts[here, :], images[rows:, :], (1, 1)))
-
-    lax.fori_loop(0, IMAGE_PARTS, corner_step, None)
-
-    def back_step(k, _):
-        for part in range(TEXT_PARTS // IMAGE_PARTS):
-            j = k * (TEXT_PARTS // IMAGE_PARTS) + part
-            text_send[text_rows(j), :] = product(weights[text_rows(j, visit), :], images[...], (1, 0)).astype(BF16)
-            pl.when(even)(lambda: text_back_copy(j).start())
-            pl.when(odd)(lambda: via_back_copy(j).start())
-            if part == 0:
-                there = image_rows(k, rows)
-                image_send[image_rows(k), :] = product(
-                    weights[: 2 * rows, there], texts[: 2 * rows, :], (0, 0)
-                ).astype(BF16)
-                image_back_copy(k).start()
-
-    lax.fori_loop(0, IMAGE_PARTS, back_step, None)
-
-    def rest_step(k, _):
-        here = image_rows(k)
-        text_acc[here, :] = product(weights[here, :], images[...], (1, 0))
-        image_acc[here, :] = product(weights[:, here], texts[...], (0, 0))
-
-    lax.fori_loop(0, IMAGE_PARTS, rest_step, None)
+            each(IMAGE_PARTS, lambda k: image_copy(k).start())
+
+    def relay_back_step(k, _):
+        mine = text_rows(k)
+        via_back_copy(k).wait_recv()
+        group_send[mine, :] = (group_acc[mine, :] + relay_back[mine, :].astype(F32)).astype(BF16)
+        sum_back_copy(k).start()
+        pl.when(k + AHEAD < TEXT_PARTS)(lambda: text_back_copy(k + AHEAD).start())
 
     def project(raw, inv, accum, where):
         inverse = inv[where, :]
         unit = raw[where, :] * inverse
         raw[where, :] = inverse * (accum - unit * jnp.sum(unit * accum, axis=-1, keepdims=True))
 
-    def last_step(k, _):
-        for part in range(TEXT_PARTS // IMAGE_PARTS):
-            j = k * (TEXT_PARTS // IMAGE_PARTS) + part
-            here = text_rows(j)
-
-            @pl.when(even)
-            def _():
-                via_back_copy(j).wait_recv()
-                group_send[here, :] = (group_acc[here, :] + relay_back[here, :].astype(F32)).astype(BF16)
-                sum_back_copy(j).start()
-                group_back_copy(j).wait_recv()
-                text_acc[here, :] += group_back[here, :].astype(F32)
-
-            text_back_copy(j).wait_recv()
-            project(text32, text_inv, text_acc[here, :] + text_back[here, :].astype(F32), here)
-            text_store(j).start()
+    def text_last(k):
+        here = text_rows(k)
+
+        @pl.when(even)
+        def _():
+            group_back_copy(k).wait_recv()
+            text_acc[here, :] += group_back[here, :].astype(F32)
+
+        text_back_copy(k).wait_recv()
+        project(text32, text_inv, text_acc[here, :] + text_back[here, :].astype(F32), here)
+        text_store(k).start()
+
+    def image_last(k, _):
         here = image_rows(k)
         image_back_copy(k).wait_recv()
         project(image32, image_inv, image_acc[here, :] + image_back[here, :].astype(F32), here)
         image_store(k).start()
 
-    lax.fori_loop(0, IMAGE_PARTS, last_step, None)
+    def image_sum(k):
+        here = image_rows(k)
+        image_acc[here, :] = product(weights[:, here], texts[...], (0, 0))
+
+    @pl.when(odd)
+    def _():
+        each(TEXT_PARTS, lambda k: group_copy(k).wait_recv())
+        for h in range(2):
+            group_send[pl.ds(h * half, half), :] = guest_half(h).astype(BF16)
+        each(TEXT_PARTS, lambda k: group_back_copy(k).start())
+        images_arrive(0)
+        images_arrive(1)
+        score(own, rows, rows, rows)
+        texts_arrive(0)
+        score(visit, half, 0, 2 * rows)
+        text_return(0)
+        texts_arrive(1)
+        score(visit + half, half, 0, 2 * rows)
+        text_return(1)
+        pl.when(odd_place)(lambda: each(TEXT_PARTS, lambda k: via_back_copy(k).start()))
+        image_return(0)
+        image_return(1)
+        pl.when(even_place)(lambda: each(IMAGE_PARTS, lambda k: image_back_copy(k).start()))
+        text_acc[...] = product(weights[:rows, :], images[...], (1, 0))
+        pl.semaphore_wait(go_sem, 1)
+        pl.when(even_place)(lambda: each(TEXT_PARTS, lambda k: via_back_copy(k).start()))
+        pl.when(odd_place)(lambda: each(IMAGE_PARTS, lambda k: image_back_copy(k).start()))
+
+        lax.fori_loop(0, IMAGE_PARTS, lambda k, _: image_sum(k), None)
+        lax.fori_loop(0, TEXT_PARTS - 1, lambda k, _: text_last(k), None)
+        lax.fori_loop(0, IMAGE_PARTS, image_last, None)
+        text_last(TEXT_PARTS - 1)
+
+    @pl.when(even)
+    def _():
+        for h in range(2):
+            lax.fori_loop(h * TEXT_PARTS // 2, (h + 1) * TEXT_PARTS // 2, relay_step, None)
+            if h == 1:
+                each(TEXT_PARTS - 1, lambda k: relay_copy(k).wait_send())
+                each(TEXT_PARTS, lambda k: direct_copy(k).start())
+            group_acc[pl.ds(h * half, half), :] = guest_half(h)
+        images_arrive(0)
+        score(own, rows, rows, half)
+        texts_arrive(0)
+        score(visit, half, 0, rows + half)
+        relay_copy(TEXT_PARTS - 1).wait_send()
+        each(TEXT_PARTS, lambda k: direct_copy(k).wait_send())
+        pl.when(even_place)(lambda: signal(go_sem, ((0, 2), (1, 2))))
+        pl.when(odd_place)(lambda: signal(go_sem, ((1, 0),)))
+        images_arrive(1)
+        score(visit, half, rows + half, half)
+        text_return(0)
+        pl.when(even_place)(lambda: pl.semaphore_wait(go_sem, 1))
+        each(AHEAD, lambda k: text_back_copy(k).start())
+        score(own, rows, rows + half, half)
+        texts_arrive(1)
+        score(visit + half, half, 0, 2 * rows)
+        text_return(1)
+        relay_back_step(0, None)
+        relay_back_step(1, None)
+        image_return(0)
+        each(IMAGE_PARTS // 2, lambda k: image_back_copy(k).start())
+        relay_back_step(2, None)
+        image_return(1)
+        each(IMAGE_PARTS // 2, lambda k: image_back_copy(k + IMAGE_PARTS // 2).start())
+        relay_back_step(3, None)
+        text_acc[...] = product(weights[:rows, :], images[...], (1, 0))
+
+        def even_step(k, _):
+            relay_back_step(k + TEXT_PARTS - IMAGE_PARTS, None)
+            image_sum(k)
+            text_last(k)
+
+        lax.fori_loop(0, IMAGE_PARTS, even_step, None)
+        lax.fori_loop(IMAGE_PARTS, TEXT_PARTS - 1, lambda k, _: text_last(k), None)
+        lax.fori_loop(0, IMAGE_PARTS, image_last, None)
+        text_last(TEXT_PARTS - 1)
 
     def text_done(k, _):
         group_copy(k).wait_send()
         text_back_copy(k).wait_send()
         group_back_copy(k).wait_send()
 
-        @pl.when(even)
-        def _():
-            direct_copy(k).wait_send()
-            relay_copy(k).wait_send()
 
         text_store(k).wait()
 
@@ -281,7 +351,7 @@
             bf, bf, bf, bf, bf, bf, bf,
             pltpu.SemaphoreType.DMA((2, TEXT_PARTS)), pltpu.SemaphoreType.DMA((2, TEXT_PARTS)),
             text_sem, text_sem, text_sem, image_sem, text_sem, image_sem, text_sem,
-            text_sem, text_sem, image_sem, text_sem, image_sem, text_sem, text_sem,
+            text_sem, text_sem, image_sem, text_sem, image_sem, text_sem, text_sem, pltpu.SemaphoreType.REGULAR, pltpu.SemaphoreType.REGULAR,
         ],
         cost_estimate=pl.CostEstimate(
             flops=15 * tile, bytes_accessed=16 * rows * width, transcendentals=5 * rows * rows

time: 83.5 us -> 80.5 us (0.964); the launches traced: 83.4 us -> 79.5 us
  Pallas kernels: 78.6 us -> 74.8 us
    pallas_call x1, Pallas kernels: 78.6 us -> 74.8 us  [local(): pl.pallas_call(functools.partial(kernel, n_grp, n_blk, rows), out_shape=(...]
where the time goes in v2:
time: 80.5 us; the launch traced here: 79.5 us
  Pallas kernels  74.8 us (93%)
  local copies, waits for them, and re-layouts  2.81 us (3%)
  between operations  1.93 us (2%)
    pallas_call x1, Pallas kernels, local(): pl.pallas_call(functools.partial(kernel, n_grp, n_blk, rows), out_shape=(...  74.8 us
    unnamed x2, local copies, waits for them, and re-layouts  2.81 us

profile of v2, /device:TPU:1, one launch (start us, length us, event | category | flops | bytes accessed | tf_op | source)
XLA Modules:
  0.0 79.5 jit_solution(14613024507672300207)
XLA Ops:
  1.9 74.8 %contrast.1 = (f32[512,1152]{1,0:T(8,128)S(1)}, f32[512,1152]{1,0:T(8,128)S(1)}) custom-call(f32[1]{0:T(128)S(6)} %copy.8.scale_ref, f32[1]{0:T(128)S(6)} %copy.9.bias_ref, f32[512,1152]{1,0:T(8,128)} %image_hbm.1, f32[512,1152]{1,0:T(8,128)} %text_hbm.1), custom_call_target="tpu_custom_call" | custom-call | flops 9059696640 | bytes 9437184 | tf_op jit(solution)/shard_map/contrast/pallas_call | solution.py:342
  76.7 1.4 %copy.10 = f32[512,1152]{1,0:T(8,128)} copy(f32[512,1152]{1,0:T(8,128)S(1)} %get-tuple-element.4) | data formatting | bytes 4718592
  78.1 1.4 %copy.11 = f32[512,1152]{1,0:T(8,128)} copy(f32[512,1152]{1,0:T(8,128)S(1)} %get-tuple-element.5) | data formatting | bytes 4718592

commit v3 on v2

--- a/solution.py
+++ b/solution.py
@@ -333,13 +333,26 @@
     lax.fori_loop(0, IMAGE_PARTS, image_done, None)
 
 
+def hand_over(rows, image_in, text_in, image_out, text_out, sem):
+    part = rows // IMAGE_PARTS
+    copies = [
+        pltpu.make_async_copy(src.at[pl.ds(k * part, part)], dst.at[pl.ds(k * part, part)], sem.at[i, k])
+        for i, (src, dst) in enumerate(((image_in, image_out), (text_in, text_out)))
+        for k in range(IMAGE_PARTS)
+    ]
+    for copy in copies:
+        copy.start()
+    for copy in copies:
+        copy.wait()
+
+
 def local(n_grp, n_blk, image_emb, text_emb, logit_scale, logit_bias):
     rows, width = image_emb.shape
     whole, bf = pltpu.VMEM((rows, width), F32), pltpu.VMEM((rows, width), BF16)
     text_sem, image_sem = pltpu.SemaphoreType.DMA((TEXT_PARTS,)), pltpu.SemaphoreType.DMA((IMAGE_PARTS,))
     out = jax.ShapeDtypeStruct((rows, width), F32)
     tile = 2 * rows * rows * width
-    return pl.pallas_call(
+    grads = pl.pallas_call(
         functools.partial(kernel, n_grp, n_blk, rows),
         out_shape=(out, out),
         in_specs=[pl.BlockSpec(memory_space=pltpu.SMEM)] * 2 + [pl.BlockSpec(memory_space=pl.ANY)] * 2,
@@ -363,6 +376,18 @@
     )(logit_scale, logit_bias, image_emb, text_emb)
 
 
+    return pl.pallas_call(
+        functools.partial(hand_over, rows),
+        out_shape=(out, out),
+        in_specs=[pl.BlockSpec(memory_space=pl.ANY)] * 2,
+        out_specs=(pl.BlockSpec(memory_space=pl.ANY),) * 2,
+        scratch_shapes=[pltpu.SemaphoreType.DMA((2, IMAGE_PARTS))],
+        cost_estimate=pl.CostEstimate(flops=0, bytes_accessed=8 * rows * width, transcendentals=0),
+        compiler_params=pltpu.CompilerParams(vmem_limit_bytes=2**20),
+        name="hand_over",
+    )(*grads)
+
+
 def solution(mesh):
     blocks = P(("grp", "blk"), None)
     return jax.shard_map(

time: 80.5 us -> 80.1 us (level)
  local copies, waits for them, and re-layouts: 2.81 us -> 0 us
  Pallas kernels: 74.8 us -> 77 us
    unnamed x2 -> x0, local copies, waits for them, and re-layouts: 2.81 us -> none
    pallas_call x0 -> x1, Pallas kernels: none -> 2.25 us  [local(): pl.pallas_call(functools.partial(hand_over, rows), out_shape=(out, out),...]
where the time goes in v3:
time: 80.1 us; the launch traced here: 79.2 us
  Pallas kernels  77 us (96%)
  between operations  2.11 us (3%)
    pallas_call x1, Pallas kernels, local(): pl.pallas_call(functools.partial(kernel, n_grp, n_blk, rows), out_shape=(...  74.8 us
    pallas_call x1, Pallas kernels, local(): pl.pallas_call(functools.partial(hand_over, rows), out_shape=(out, out),...  2.25 us

profile of v3, /device:TPU:1, one launch (start us, length us, event | category | flops | bytes accessed | tf_op | source)
XLA Modules:
  0.0 79.2 jit_solution(4607218969214823317)
XLA Ops:
  1.9 74.8 %contrast.1 = (f32[512,1152]{1,0:T(8,128)S(1)}, f32[512,1152]{1,0:T(8,128)S(1)}) custom-call(f32[1]{0:T(128)S(6)} %copy.6.scale_ref, f32[1]{0:T(128)S(6)} %copy.7.bias_ref, f32[512,1152]{1,0:T(8,128)} %image_hbm.1, f32[512,1152]{1,0:T(8,128)} %text_hbm.1), custom_call_target="tpu_custom_call" | custom-call | flops 9059696640 | bytes 9437184 | tf_op jit(solution)/shard_map/contrast/pallas_call | solution.py:355
  76.7 2.2 %hand_over.1 = (f32[512,1152]{1,0:T(8,128)}, f32[512,1152]{1,0:T(8,128)}) custom-call(f32[512,1152]{1,0:T(8,128)S(1)} %get-tuple-element.4.image_in, f32[512,1152]{1,0:T(8,128)S(1)} %get-tuple-element.5.text_in), custom_call_target="tpu_custom_call" | custom-call | bytes 4718592 | tf_op jit(solution)/shard_map/hand_over/pallas_call | solution.py:379
